TPU v7x, 256 devices: a whole 4x4x8 slice. The times are simulated.
256 devices in a mesh: sect: 8 (over y, core), dev: 32 (over z, x).
Axes of the slice: x: 4, y: 4, z: 8, core: 2. Of those that a mesh axis runs over, the one named last changes fastest.
Arguments:
- prompt_lengths: int32 [8, 256], P(None, 'dev'), may hold values from 64 to 128, as said below
- owner_map: int32 [8, 256], P(None, 'dev'), may hold values from 0 to 63, as said below
- block_table: int32 [8, 256, 2], P(None, 'dev'), may hold values from 0 to 15, as said below
- pool_blocks: bfloat16 [8, 512, 64, 576], P('sect', 'dev'), may hold values from -4.5 to 4.5
- queries: bfloat16 [4, 2048, 128, 576], P(None, ('sect', 'dev')), may hold values from -48 to 48
- new_latents: bfloat16 [4, 2048, 576], P(None, ('sect', 'dev')), may hold values from -4.5 to 4.5
- value_up: bfloat16 [128, 512, 128], P('dev'), may hold values from -1.5 to 1.5
- out_proj: bfloat16 [16384, 7168], P('dev'), may hold values from -0.046875 to 0.046875
Outputs:
- decoded: bfloat16 [4, 2048, 7168], P(None, ('sect', 'dev'))
Inputs may be any that keep to these rules, and one draw needn't show every extreme that they name: `prompt_lengths`: in each section some request has length 128. Within each device index d, the entries owner_map[p, d * 8 + i] over all p and i name every decode slot 0 to 63 once, and the 8 requests of one section and device index name 8 different sections g. `block_table`: the entries of the 8 requests of one section and device index form a permutation of 0 to 15.
All inputs are finite; a program needn't handle non-finite values.
Results may differ from a plain program's by a relative error of at most 0.02.
Values may be sent and summed in bfloat16 or wider, within the bound.
A program may use at most 128 MiB of HBM per device.

v0:
```python
import jax
import jax.numpy as jnp
from jax import lax
from jax.experimental import pallas as pl
from jax.experimental.pallas import tpu as pltpu
from jax.sharding import PartitionSpec as P

MESH = pl.DeviceIdType.MESH
CHIPS_X = 4
GROUP = 2
score_scale = 192.0 ** (-0.5)
masked_score = -1e30


def ilog2(n):
    return n.bit_length() - 1


def tn_dot(a, b):
    return lax.dot_general(a, b, (((0,), (0,)), ((), ())), preferred_element_type=jnp.float32)


def mm(a, b):
    return jnp.dot(a, b, preferred_element_type=jnp.float32)


def make_kernel(sections, chips_z, chips_x, steps, req, heads, lat_w, width, vdim, model, block):
    Y, Z, X = sections // 2, chips_z, chips_x
    HD = heads // (Z * X)
    HZ = HD * X
    NG = req // GROUP
    NPG = NG // 2
    PS = GROUP * steps
    CR = 2 * block
    KR = CR + 16
    PAIRS = X // 2
    NX = model // 2
    HX = NX // 2
    PR = 2 * PS
    NT = 256
    KD = HD * vdim
    PW = KD // (2 * Y)

    def kernel(
        owner_ref, table_ref, len_ref, pool_hbm, q_hbm, new_ref, vu_hbm, op_hbm, out_ref,
        pool, q, pk, keys, lat, snd, rcv, vu, val, vz, va, w, po, rs, so, fin,
        lsem, cs, cr, v1s, v1r, v3s, v3r, w1s, w1r, w2s, w2r, w3s, w3r,
        ls, lr, zs, zr, gs, gr, ss, sr, fs, fr,
    ):
        sect = lax.axis_index("sect")
        dev = lax.axis_index("dev")
        y, c = sect // 2, sect % 2
        z, x = dev // X, dev % X
        sibling = y * 2 + (1 - c)
        piece = c * Y + y
        pair, half = x // 2, x % 2
        sends = []

        hops = [(0, 0), (0, 1), (1, 0), (Y - 1, 0), (1, 1), (Y - 1, 1), (2, 0), (2, 1)]
        if Y == 2:
            hops = [(0, 0), (0, 1), (1, 0), (1, 1)]

        def hop(k):
            if isinstance(k, int):
                return hops[k]
            over, across = jnp.int32(0), jnp.int32(0)
            for i, (a, b) in enumerate(hops):
                over += jnp.where(k == i, a, 0)
                across += jnp.where(k == i, b, 0)
            return over, across

        def at_sect(k):
            over, across = hops[k]
            return ((y + over) % Y * 2 + (c + across) % 2, dev)

        def at_y(r):
            return (((y + r) % Y) * 2 + c, dev)

        def at_z(r):
            return (sect, ((z + r) % Z) * X + x)

        def at_x(r):
            return (sect, z * X + (x + r) % X)

        def remote(src, dst, send_sem, recv_sem, to):
            return pltpu.make_async_remote_copy(
                src_ref=src, dst_ref=dst, send_sem=send_sem, recv_sem=recv_sem,
                device_id=to, device_id_type=MESH,
            )

        def send(src, dst, send_sem, recv_sem, to):
            copy = remote(src, dst, send_sem, recv_sem, to)
            copy.start()
            sends.append(copy)

        def arrived(src, dst, send_sem, recv_sem, to):
            remote(src, dst, send_sem, recv_sem, to).wait_recv()

        load_pool = pltpu.make_async_copy(pool_hbm.at[0], pool, lsem.at[0])
        load_q = pltpu.make_async_copy(q_hbm, q, lsem.at[1])
        load_vu = pltpu.make_async_copy(vu_hbm, vu.at[0], lsem.at[2])
        own_cols = pl.ds(pl.multiple_of(half * NX, 128), NX)
        load_w = pltpu.make_async_copy(op_hbm.at[:, own_cols], w.at[0], lsem.at[3])
        load_pool.start()
        load_q.start()
        load_vu.start()
        load_w.start()

        barrier = pltpu.get_barrier_semaphore()
        peers = [at_sect(r) for r in range(1, sections)]
        peers += [at_z(r) for r in range(1, Z)] + [at_x(r) for r in range(1, X)]
        for peer in peers:
            pl.semaphore_signal(barrier, inc=1, device_id=peer, device_id_type=MESH)

        new_rows = new_ref[...].astype(jnp.float32).reshape(steps * req, width)
        new_rows = new_rows.astype(jnp.bfloat16)
        pick_u = lax.broadcasted_iota(jnp.int32, (16, steps * req), 0)
        pick_i = lax.broadcasted_iota(jnp.int32, (16, steps * req), 1)

        def slot_and_length(k):
            over, across = hop(k)
            source = lax.rem(y - over + Y, Y) * 2 + lax.rem(c + across, 2)
            slot, length = jnp.int32(0), jnp.int32(0)
            for i in range(req):
                owner = owner_ref[source, i]
                mine = lax.div(owner, req) == sect
                slot += jnp.where(mine, lax.rem(owner, req), 0)
                length += jnp.where(mine, len_ref[source, i], 0)
            return slot, length

        def fresh(k, carry):
            slot, _ = slot_and_length(k)
            pick = (pick_u == (pick_i >> ilog2(req))) & ((pick_i & (req - 1)) == slot)
            rows = mm(pick.astype(jnp.bfloat16), new_rows)
            keys[k, pl.ds(CR, 16), :] = rows.astype(jnp.bfloat16)
            return carry

        lax.fori_loop(0, req, fresh, 0)
        load_pool.wait()

        def pack(r):
            over, across = hop(r)
            target = lax.rem(y + over, Y) * 2 + lax.rem(c + across, 2)
            first, second = jnp.int32(0), jnp.int32(0)
            for i in range(req):
                hit = lax.div(owner_ref[sect, i], req) == target
                first += jnp.where(hit, table_ref[sect, 0, i], 0)
                second += jnp.where(hit, table_ref[sect, 1, i], 0)
            return pool[first], pool[second]

        def pack_remote(r, carry):
            a, b = pack(r)
            pk[r, 0:block, :] = a
            pk[r, block:CR, :] = b
            return carry

        lax.fori_loop(1, sections, pack_remote, 0)
        a, b = pack(0)
        keys[0, 0:block, :] = a
        keys[0, block:CR, :] = b

        pl.semaphore_wait(barrier, len(peers))

        def cache_args(r):
            return pk.at[r], keys.at[r, pl.ds(0, CR), :], cs.at[r], cr.at[r], at_sect(r)

        for r in range(1, sections):
            send(*cache_args(r))

        wrows = pl.ds(pl.multiple_of(piece * PW, PW), PW)

        VH = lat_w // 2
        ways = Z // 2

        def core_rows(core):
            return pl.ds(pl.multiple_of(core * VH, VH), VH)

        def v1_args(h, d):
            sign = 1 - 2 * d
            some = pl.ds(d * (HD // 2), HD // 2) if h == ways else pl.ds(0, HD)
            rows = core_rows(c)
            if h == 1:
                part = vu_hbm.at[some, rows, :]
            else:
                part = vu.at[sign * (h - 1) % Z, some, rows, :]
            return part, vu.at[sign * h % Z, some, rows, :], v1s.at[d, h], v1r.at[d, h], at_z(sign + Z)

        def v3_args(r, core):
            part = vu.at[r, :, core_rows(core), :]
            return part, part, v3s.at[r], v3r.at[r], (sibling, dev)

        def v_step(h):
            if h > 1:
                for d in range(2):
                    arrived(*v1_args(h - 1, d))
            if h <= ways:
                for d in range(2):
                    send(*v1_args(h, d))
            if 1 < h <= ways:
                for r in (h - 1, Z - h + 1):
                    send(*v3_args(r, c))
            if h == ways + 1:
                send(*v3_args(ways, c))

        def w1_args(r):
            cols = pl.ds(pl.multiple_of(((x + r) % X) % 2 * NX, 128), NX)
            return op_hbm.at[wrows, cols], w.at[r, wrows, :], w1s.at[r], w1r.at[r], at_x(r)

        def from_y(r, size, part, parts):
            start = (c * Y + (y - r + Y) % Y) * size + part * (size // parts)
            return pl.ds(pl.multiple_of(start, size // parts), size // parts)

        def w2_args(r, rows, slot):
            part = w.at[pl.ds(1, X - 1), rows, :]
            return part, part, w2s.at[slot], w2r.at[slot], at_y(r)

        def y_start(args, size):
            send(*args(1, from_y(0, size, 0, 1), 0))
            if Y > 2:
                send(*args(Y - 1, from_y(0, size, 0, 1), 1))

        def w3_args(r, core):
            rows = pl.ds(pl.multiple_of((core * Y + (y - r + Y) % Y) * PW, PW), PW)
            part = w.at[pl.ds(1, X - 1), rows, :]
            return part, part, w3s.at[r], w3r.at[r], (sibling, dev)

        def y_forward(args, size, across):
            send(*across(0, c))
            arrived(*args(1, from_y(1, size, 0, 1), 0))
            if Y > 2:
                send(*args(1, from_y(1, size, 0, 2), 2))
                arrived(*args(Y - 1, from_y(Y - 1, size, 0, 1), 1))
                send(*args(Y - 1, from_y(Y - 1, size, 1, 2), 3))
                send(*across(Y - 1, c))
            send(*across(1, c))

        def y_finish(args, size, across):
            if Y > 2:
                arrived(*args(1, from_y(2, size, 0, 2), 2))
                arrived(*args(Y - 1, from_y(2, size, 1, 2), 3))
                send(*across(2, c))

        v_step(1)
        for r in range(1, X):
            send(*w1_args(r))

        swap_out = lax.broadcasted_iota(jnp.int32, (HZ * PS, HZ * PS), 0)
        swap_in = lax.broadcasted_iota(jnp.int32, (HZ * PS, HZ * PS), 1)
        swap = ((swap_out >> ilog2(PS)) == (swap_in & (HZ - 1))) & (
            (swap_out & (PS - 1)) == (swap_in >> ilog2(HZ))
        )
        swap = swap.astype(jnp.bfloat16)
        load_q.wait()

        def attend(k, k4):
            slot, length = slot_and_length(k)
            key_rows = keys[k]
            key_lat = keys[k, :, 0:lat_w]
            q_cols = jnp.concatenate([q[s, slot] for s in range(steps)], axis=1)
            scores = mm(key_rows, q_cols) * score_scale
            row = lax.broadcasted_iota(jnp.int32, scores.shape, 0)
            step = lax.broadcasted_iota(jnp.int32, scores.shape, 1) >> ilog2(heads)
            held = jnp.where(row < CR, length, CR + 1 + step)
            scores = jnp.where(row < held, scores, masked_score)
            weights = jnp.exp(scores - jnp.max(scores, axis=0, keepdims=True))
            probs = weights * (1.0 / jnp.sum(weights, axis=0, keepdims=True))
            out = tn_dot(probs.astype(jnp.bfloat16), key_lat).astype(jnp.bfloat16)
            lat[k4] = out.reshape(steps, heads, lat_w)

        def latent_args(r, pg):
            to = (x + r) % X
            return snd.at[to, pg], rcv.at[x, pg], ls.at[pg, r], lr.at[pg, r], at_x(r)

        def latent_from(r, pg):
            source = (x - r + X) % X
            return snd.at[source, pg], rcv.at[source, pg], ls.at[pg, r], lr.at[pg, r], at_x(r)

        local_latents = []

        def attention(pg):
            def one(k4, carry):
                k = pg * GROUP + k4

                @pl.when(k > 0)
                def _():
                    arrived(pk.at[k], keys.at[k, pl.ds(0, CR), :], cs.at[k], cr.at[k], at_sect(1))

                attend(k, k4)
                return carry

            lax.fori_loop(0, GROUP, one, 0)

            def turn(zz, carry):
                part = lat[:, :, pl.ds(pl.multiple_of(zz * HZ, HZ), HZ), :]
                turned = mm(swap, part.reshape(PS * HZ, lat_w)).astype(jnp.bfloat16)
                snd[:, pg, zz] = turned.reshape(X, HD * PS, lat_w)
                return carry

            lax.fori_loop(0, Z, turn, 0)
            for r in range(1, X):
                send(*latent_args(r, pg))
            own = pltpu.make_async_copy(snd.at[x, pg], rcv.at[x, pg], lsem.at[4 + pg])
            own.start()
            local_latents.append(own)

        def value_args(r, pg):
            to = (z + r) % Z
            return val.at[to, pg], vz.at[pg, :, z], zs.at[pg, r], zr.at[pg, r], at_z(r)

        def value_from(r, pg):
            source = (z - r + Z) % Z
            return val.at[source, pg], vz.at[pg, :, source], zs.at[pg, r], zr.at[pg, r], at_z(r)

        local_values = []

        def values(pg):
            for r in range(1, X):
                arrived(*latent_from(r, pg))
            local_latents[pg].wait()

            def ring(r, carry):
                zz = lax.rem(z - r + Z, Z)
                maps = jnp.concatenate([vu[r, hh] for hh in range(HD)], axis=1)
                full = mm(rcv[:, pg, zz].reshape(X * HD * PS, lat_w), maps)
                full = full.reshape(X, HD, PS, KD)
                for hh in range(HD):
                    cols = slice(hh * vdim, (hh + 1) * vdim)
                    part = full[:, hh, :, cols].reshape(PAIRS, PR, vdim).astype(jnp.bfloat16)
                    val[zz, pg, :, :, cols] = part
                return carry

            lax.fori_loop(0, Z, ring, 0)
            for r in range(1, Z):
                send(*value_args(r, pg))
            own = pltpu.make_async_copy(val.at[z, pg], vz.at[pg, :, z], lsem.at[4 + NG + pg])
            own.start()
            local_values.append(own)

        def gather_args(r, pg):
            to = ((x + r) % X) // 2
            return vz.at[pg, to], va.at[r, pg], gs.at[pg, r], gr.at[pg, r], at_x(r)

        def gather_start(pg):
            for r in range(1, Z):
                arrived(*value_from(r, pg))
            local_values[pg].wait()
            for r in range(1, X):
                send(*gather_args(r, pg))

        def ring_args(d, i, g):
            sign = 1 - 2 * d
            target = (z - sign * (1 + i) + Z) % Z
            held = po.at[target, g, d] if i == 0 else rs.at[d, g, i - 1]
            return held, rs.at[d, g, i], ss.at[d, g, i], sr.at[d, g, i], at_z(sign + Z)

        def ring_step(i, g):
            for d in range(2):
                arrived(*ring_args(d, i - 1, g))
                target = (z - (1 - 2 * d) * (1 + i) + 2 * Z) % Z
                total = rs[d, g, i - 1].astype(jnp.float32)
                total += po[target, g, d].astype(jnp.float32)
                rs[d, g, i - 1] = total.astype(jnp.bfloat16)
                send(*ring_args(d, i, g))

        def project(g):
            for r in range(1, X):
                arrived(*gather_args(r, g))
            for d in range(2):

                def tile(n, carry):
                    cols = pl.ds(pl.multiple_of(d * HX + n * NT, NT), NT)
                    acc = mm(vz[g, pair].reshape(Z * PR, KD), w[0, :, cols])
                    for r in range(1, X):
                        acc += mm(va[r, g].reshape(Z * PR, KD), w[r, :, cols])
                    part = acc.astype(jnp.bfloat16).reshape(Z, PR, NT)
                    po[:, g, d, :, pl.ds(pl.multiple_of(n * NT, NT), NT)] = part
                    return carry

                lax.fori_loop(0, HX // NT, tile, 0)
                send(*ring_args(d, 0, g))

        def final_args(pg, side):
            return so.at[pg, 1 - side], fin.at[side, pg], fs.at[pg], fr.at[pg], at_x(1 - 2 * half + X)

        local_final = []

        def reduce(pg):
            for d in range(2):
                totals = []
                for g in (2 * pg, 2 * pg + 1):
                    arrived(*ring_args(d, Z - 2, g))
                    total = po[z, g, d].astype(jnp.float32)
                    totals.append(total + rs[d, g, Z - 2].astype(jnp.float32))
                for m in range(2):
                    rows = jnp.concatenate([t[m * PS : (m + 1) * PS] for t in totals], axis=0)
                    so[pg, m, :, pl.ds(d * HX, HX)] = rows.astype(jnp.bfloat16)
            send(*final_args(pg, half))
            own = pltpu.make_async_copy(so.at[pg, half], fin.at[half, pg], lsem.at[4 + 2 * NG + pg])
            own.start()
            local_final.append(own)

        step = 2
        for g in range(NG):
            attention(g)
            if g != 1 and step <= ways:
                v_step(step)
                step += 1
        for r in range(1, X):
            arrived(*w1_args(r))
        y_start(w2_args, PW)
        while step <= ways + 1:
            v_step(step)
            step += 1
        load_vu.wait()
        for r in range(1, Z):
            arrived(*v3_args(r, 1 - c))
        for g in range(NG):
            values(g)
            if g:
                gather_start(g - 1)
            if g == 1:
                y_forward(w2_args, PW, w3_args)
            if g == NG - 2:
                y_finish(w2_args, PW, w3_args)
        load_w.wait()
        for r in range(Y):
            arrived(*w3_args(r, 1 - c))
        project(0)
        gather_start(NG - 1)
        rings = [1]
        while min(rings) < Z:
            started = len(rings)
            if started < NG:
                project(started)
            for g in range(started):
                if rings[g] < Z - 1:
                    ring_step(rings[g], g)
                elif rings[g] == Z - 1 and g % 2:
                    reduce(g // 2)
                rings[g] += 1
            if started < NG:
                rings.append(1)

        place_out = lax.broadcasted_iota(jnp.int32, (steps * req, steps * req), 0)
        place_in = lax.broadcasted_iota(jnp.int32, (steps * req, steps * req), 1)
        slots = jnp.zeros((steps * req, steps * req), jnp.int32)
        for k in range(req):
            slot, _ = slot_and_length(k)
            slots = jnp.where((place_in >> ilog2(steps)) == k, slot, slots)
        place = ((place_out >> ilog2(req)) == (place_in & (steps - 1))) & (
            (place_out & (req - 1)) == slots
        )
        place = place.astype(jnp.bfloat16)
        for pg in range(NPG):
            arrived(*final_args(pg, 1 - half))
            local_final[pg].wait()
        for side in range(2):
            rows = mm(place, fin[side].reshape(steps * req, NX))
            for s in range(steps):
                part = rows[s * req : (s + 1) * req].astype(jnp.bfloat16)
                out_ref[s, :, side * NX : (side + 1) * NX] = part

        for copy in sends:
            copy.wait_send()

    bf = jnp.bfloat16
    dma = pltpu.SemaphoreType.DMA
    scratch = [
        pltpu.VMEM((2 * req, block, width), bf),
        pltpu.VMEM((steps, req, width, heads), bf),
        pltpu.VMEM((sections, CR, width), bf),
        pltpu.VMEM((req, KR, width), bf),
        pltpu.VMEM((GROUP, steps, heads, lat_w), bf),
        pltpu.VMEM((X, NG, Z, HD * PS, lat_w), bf),
        pltpu.VMEM((X, NG, Z, HD * PS, lat_w), bf),
        pltpu.VMEM((Z, HD, lat_w, vdim), bf),
        pltpu.VMEM((Z, NG, PAIRS, PR, KD), bf),
        pltpu.VMEM((NG, PAIRS, Z, PR, KD), bf),
        pltpu.VMEM((X, NG, Z, PR, KD), bf),
        pltpu.VMEM((X, KD, NX), bf),
        pltpu.VMEM((Z, NG, 2, PR, HX), bf),
        pltpu.VMEM((2, NG, Z - 1, PR, HX), bf),
        pltpu.VMEM((NPG, 2, 2 * PS, NX), bf),
        pltpu.VMEM((2, NPG, 2 * PS, NX), bf),
        dma((4 + 2 * NG + NPG,)),
        dma((sections,)), dma((sections,)),
        dma((2, Z)), dma((2, Z)), dma((Z,)), dma((Z,)),
        dma((X,)), dma((X,)), dma((4,)), dma((4,)), dma((Y,)), dma((Y,)),
        dma((NG, X)), dma((NG, X)), dma((NG, Z)), dma((NG, Z)),
        dma((NG, X)), dma((NG, X)), dma((2, NG, Z)), dma((2, NG, Z)),
        dma((NPG,)), dma((NPG,)),
    ]
    return kernel, scratch


def on_device(
    prompt_lengths, owner_map, block_table, pool_blocks, queries, new_latents, value_up, out_proj
):
    sections, devices = lax.axis_size("sect"), lax.axis_size("dev")
    steps, req, heads, width = queries.shape
    _, lat_w, vdim = value_up.shape
    model = out_proj.shape[1]
    block = pool_blocks.shape[2]
    kernel, scratch = make_kernel(
        sections, devices // CHIPS_X, CHIPS_X, steps, req, heads, lat_w, width, vdim, model, block
    )
    smem = pl.BlockSpec(memory_space=pltpu.SMEM)
    vmem = pl.BlockSpec(memory_space=pltpu.VMEM)
    hbm = pl.BlockSpec(memory_space=pl.ANY)
    return pl.pallas_call(
        kernel,
        out_shape=jax.ShapeDtypeStruct((steps, req, model), jnp.bfloat16),
        in_specs=[smem, smem, smem, hbm, hbm, vmem, hbm, hbm],
        out_specs=vmem,
        scratch_shapes=scratch,
        compiler_params=pltpu.CompilerParams(
            collective_id=0, has_side_effects=True, vmem_limit_bytes=60 * 1024 * 1024
        ),
    )(
        owner_map,
        jnp.swapaxes(block_table, 1, 2),
        prompt_lengths,
        pool_blocks,
        jnp.swapaxes(queries, 2, 3),
        new_latents,
        value_up,
        out_proj,
    )


def solution(mesh):
    in_specs = (
        P(None, "dev"),
        P(None, "dev"),
        P(None, "dev", None),
        P("sect", "dev", None, None),
        P(None, ("sect", "dev"), None, None),
        P(None, ("sect", "dev"), None),
        P("dev", None, None),
        P("dev", None),
    )
    out_specs = P(None, ("sect", "dev"), None)
    return jax.shard_map(
        on_device, mesh=mesh, in_specs=in_specs, out_specs=out_specs, check_vma=False
    )
```

profile of v0, /device:TPU:2, one launch (start us, length us, event | category | flops | bytes accessed | tf_op | source)
XLA Modules:
  0.0 147.4 jit_solution(3296318447425128971)
XLA Ops:
  0.0 145.6 %shard_map.82 = bf16[4,8,7168]{2,1,0:T(8,128)(2,1)} custom-call(s32[8,8]{1,0:T(8,128)} %owner_ref.1, s32[8,2,8]{2,1,0:T(2,128)} %bitcast.3, s32[8,8]{1,0:T(8,128)} %len_ref.1, bf16[1,16,64,576]{3,2,1,0:T(8,128)(2,1)} %pool_hbm.1, bf16[4,8,576,128]{3,2,1,0:T(8,128)(2,1)} %bitcast.2, bf16[4,8,576]{2,1,0:T(8,128)(2,1)} %new_ref.1, bf16[4,512,128]{2,1,0:T(8,128)(2,1)} %vu_hbm.1, ...), custom_call_target="tpu_custom_call" | custom-call | tf_op jit(solution)/shard_map/pallas_call | solution.py:510
  145.6 1.8 %copy.10 = bf16[4,8,7168]{2,1,0:T(8,128)(2,1)} copy(bf16[4,8,7168]{2,1,0:T(8,128)(2,1)} %shard_map.82) | data formatting | bytes 917504
where the time goes:
time: 148 us; the launch traced here: 147 us
  Pallas kernels  146 us (99%)
  local copies, waits for them, and re-layouts  1.82 us (1%)
    pallas_call x1, Pallas kernels, on_device(): pl.pallas_call(kernel, out_shape=jax.ShapeDtypeStruct((steps, req, model)...  146 us

commit v1 on v0

--- a/solution.py
+++ b/solution.py
@@ -210,19 +210,25 @@
             start = (c * Y + (y - r + Y) % Y) * size + part * (size // parts)
             return pl.ds(pl.multiple_of(start, size // parts), size // parts)
 
-        def w2_args(r, rows, slot):
-            part = w.at[pl.ds(1, X - 1), rows, :]
-            return part, part, w2s.at[slot], w2r.at[slot], at_y(r)
+        def w2_args(shard):
+            def args(r, rows, slot):
+                part = w.at[shard, rows, :]
+                return part, part, w2s.at[shard, slot], w2r.at[shard, slot], at_y(r)
+
+            return args
 
         def y_start(args, size):
             send(*args(1, from_y(0, size, 0, 1), 0))
             if Y > 2:
                 send(*args(Y - 1, from_y(0, size, 0, 1), 1))
 
-        def w3_args(r, core):
-            rows = pl.ds(pl.multiple_of((core * Y + (y - r + Y) % Y) * PW, PW), PW)
-            part = w.at[pl.ds(1, X - 1), rows, :]
-            return part, part, w3s.at[r], w3r.at[r], (sibling, dev)
+        def w3_args(shard):
+            def args(r, core):
+                rows = pl.ds(pl.multiple_of((core * Y + (y - r + Y) % Y) * PW, PW), PW)
+                part = w.at[shard, rows, :]
+                return part, part, w3s.at[shard, r], w3r.at[shard, r], (sibling, dev)
+
+            return args
 
         def y_forward(args, size, across):
             send(*across(0, c))
@@ -241,7 +247,8 @@
                 send(*across(2, c))
 
         v_step(1)
-        for r in range(1, X):
+        blocks = [1, X - 1, 2] if X > 2 else [1]
+        for r in blocks:
             send(*w1_args(r))
 
         swap_out = lax.broadcasted_iota(jnp.int32, (HZ * PS, HZ * PS), 0)
@@ -405,26 +412,35 @@
             if g != 1 and step <= ways:
                 v_step(step)
                 step += 1
-        for r in range(1, X):
+        for r in blocks[:2]:
             arrived(*w1_args(r))
-        y_start(w2_args, PW)
+            y_start(w2_args(r), PW)
         while step <= ways + 1:
             v_step(step)
             step += 1
         load_vu.wait()
         for r in range(1, Z):
             arrived(*v3_args(r, 1 - c))
+        for r in blocks[2:]:
+            arrived(*w1_args(r))
+            y_start(w2_args(r), PW)
         for g in range(NG):
             values(g)
+            if g == 0:
+                for r in blocks[:2]:
+                    y_forward(w2_args(r), PW, w3_args(r))
             if g:
                 gather_start(g - 1)
             if g == 1:
-                y_forward(w2_args, PW, w3_args)
+                for r in blocks[2:]:
+                    y_forward(w2_args(r), PW, w3_args(r))
             if g == NG - 2:
-                y_finish(w2_args, PW, w3_args)
+                for r in blocks:
+                    y_finish(w2_args(r), PW, w3_args(r))
         load_w.wait()
-        for r in range(Y):
-            arrived(*w3_args(r, 1 - c))
+        for shard in blocks:
+            for r in range(Y):
+                arrived(*w3_args(shard)(r, 1 - c))
         project(0)
         gather_start(NG - 1)
         rings = [1]
@@ -485,7 +501,7 @@
         dma((4 + 2 * NG + NPG,)),
         dma((sections,)), dma((sections,)),
         dma((2, Z)), dma((2, Z)), dma((Z,)), dma((Z,)),
-        dma((X,)), dma((X,)), dma((4,)), dma((4,)), dma((Y,)), dma((Y,)),
+        dma((X,)), dma((X,)), dma((X, 4)), dma((X, 4)), dma((X, Y)), dma((X, Y)),
         dma((NG, X)), dma((NG, X)), dma((NG, Z)), dma((NG, Z)),
         dma((NG, X)), dma((NG, X)), dma((2, NG, Z)), dma((2, NG, Z)),
         dma((NPG,)), dma((NPG,)),

time: 148 us -> 148 us (level)
  no operation moved by 1% of the time
where the time goes in v1:
time: 148 us
  Pallas kernels  146 us (99%)
  local copies, waits for them, and re-layouts  1.82 us (1%)
    pallas_call x1, Pallas kernels, on_device(): pl.pallas_call(kernel, out_shape=jax.ShapeDtypeStruct((steps, req, model)...  146 us

profile of v1, /device:TPU:2, one launch (start us, length us, event | category | flops | bytes accessed | tf_op | source)
XLA Modules:
  0.0 147.9 jit_solution(16501162125165438290)
XLA Ops:
  0.0 146.1 %shard_map.82 = bf16[4,8,7168]{2,1,0:T(8,128)(2,1)} custom-call(s32[8,8]{1,0:T(8,128)} %owner_ref.1, s32[8,2,8]{2,1,0:T(2,128)} %bitcast.3, s32[8,8]{1,0:T(8,128)} %len_ref.1, bf16[1,16,64,576]{3,2,1,0:T(8,128)(2,1)} %pool_hbm.1, bf16[4,8,576,128]{3,2,1,0:T(8,128)(2,1)} %bitcast.2, bf16[4,8,576]{2,1,0:T(8,128)(2,1)} %new_ref.1, bf16[4,512,128]{2,1,0:T(8,128)(2,1)} %vu_hbm.1, ...), custom_call_target="tpu_custom_call" | custom-call | tf_op jit(solution)/shard_map/pallas_call | solution.py:526
  146.1 1.8 %copy.10 = bf16[4,8,7168]{2,1,0:T(8,128)(2,1)} copy(bf16[4,8,7168]{2,1,0:T(8,128)(2,1)} %shard_map.82) | data formatting | bytes 917504

commit v2 on v0

--- a/solution.py
+++ b/solution.py
@@ -37,7 +37,7 @@
     NX = model // 2
     HX = NX // 2
     PR = 2 * PS
-    NT = 256
+    NT = HX // 2
     KD = HD * vdim
     PW = KD // (2 * Y)
 
@@ -365,13 +365,13 @@
         def project(g):
             for r in range(1, X):
                 arrived(*gather_args(r, g))
+            rows = [vz[g, pair]] + [va[r, g] for r in range(1, X)]
+            rows = jnp.concatenate([part.reshape(Z * PR, KD) for part in rows], axis=1)
             for d in range(2):
 
                 def tile(n, carry):
                     cols = pl.ds(pl.multiple_of(d * HX + n * NT, NT), NT)
-                    acc = mm(vz[g, pair].reshape(Z * PR, KD), w[0, :, cols])
-                    for r in range(1, X):
-                        acc += mm(va[r, g].reshape(Z * PR, KD), w[r, :, cols])
+                    acc = mm(rows, w[:, :, cols].reshape(X * KD, NT))
                     part = acc.astype(jnp.bfloat16).reshape(Z, PR, NT)
                     po[:, g, d, :, pl.ds(pl.multiple_of(n * NT, NT), NT)] = part
                     return carry

time: 148 us -> 146 us (0.986)
  Pallas kernels: 146 us -> 144 us
    pallas_call x1, Pallas kernels: 146 us -> 144 us  [on_device(): pl.pallas_call(kernel, out_shape=jax.ShapeDtypeStruct((steps, req, model)...]
where the time goes in v2:
time: 146 us
  Pallas kernels  144 us (99%)
  local copies, waits for them, and re-layouts  1.82 us (1%)
    pallas_call x1, Pallas kernels, on_device(): pl.pallas_call(kernel, out_shape=jax.ShapeDtypeStruct((steps, req, model)...  144 us

profile of v2, /device:TPU:2, one launch (start us, length us, event | category | flops | bytes accessed | tf_op | source)
XLA Modules:
  0.0 145.9 jit_solution(5023594964412012269)
XLA Ops:
  0.0 144.0 %shard_map.82 = bf16[4,8,7168]{2,1,0:T(8,128)(2,1)} custom-call(s32[8,8]{1,0:T(8,128)} %owner_ref.1, s32[8,2,8]{2,1,0:T(2,128)} %bitcast.3, s32[8,8]{1,0:T(8,128)} %len_ref.1, bf16[1,16,64,576]{3,2,1,0:T(8,128)(2,1)} %pool_hbm.1, bf16[4,8,576,128]{3,2,1,0:T(8,128)(2,1)} %bitcast.2, bf16[4,8,576]{2,1,0:T(8,128)(2,1)} %new_ref.1, bf16[4,512,128]{2,1,0:T(8,128)(2,1)} %vu_hbm.1, ...), custom_call_target="tpu_custom_call" | custom-call | tf_op jit(solution)/shard_map/pallas_call | solution.py:510
  144.0 1.8 %copy.10 = bf16[4,8,7168]{2,1,0:T(8,128)(2,1)} copy(bf16[4,8,7168]{2,1,0:T(8,128)(2,1)} %shard_map.82) | data formatting | bytes 917504

commit v3 on v2

--- a/solution.py
+++ b/solution.py
@@ -296,7 +296,7 @@
                 snd[:, pg, zz] = turned.reshape(X, HD * PS, lat_w)
                 return carry
 
-            lax.fori_loop(0, Z, turn, 0)
+            lax.fori_loop(0, Z, turn, 0, unroll=2)
             for r in range(1, X):
                 send(*latent_args(r, pg))
             own = pltpu.make_async_copy(snd.at[x, pg], rcv.at[x, pg], lsem.at[4 + pg])
@@ -329,7 +329,7 @@
                     val[zz, pg, :, :, cols] = part
                 return carry
 
-            lax.fori_loop(0, Z, ring, 0)
+            lax.fori_loop(0, Z, ring, 0, unroll=2)
             for r in range(1, Z):
                 send(*value_args(r, pg))
             own = pltpu.make_async_copy(val.at[z, pg], vz.at[pg, :, z], lsem.at[4 + NG + pg])

time: 146 us -> 146 us (level)
  no operation moved by 1% of the time
where the time goes in v3:
time: 146 us
  Pallas kernels  144 us (99%)
  local copies, waits for them, and re-layouts  1.82 us (1%)
    pallas_call x1, Pallas kernels, on_device(): pl.pallas_call(kernel, out_shape=jax.ShapeDtypeStruct((steps, req, model)...  144 us

profile of v3, /device:TPU:2, one launch (start us, length us, event | category | flops | bytes accessed | tf_op | source)
XLA Modules:
  0.0 146.0 jit_solution(7401908098763517948)
XLA Ops:
  0.0 144.2 %shard_map.82 = bf16[4,8,7168]{2,1,0:T(8,128)(2,1)} custom-call(s32[8,8]{1,0:T(8,128)} %owner_ref.1, s32[8,2,8]{2,1,0:T(2,128)} %bitcast.3, s32[8,8]{1,0:T(8,128)} %len_ref.1, bf16[1,16,64,576]{3,2,1,0:T(8,128)(2,1)} %pool_hbm.1, bf16[4,8,576,128]{3,2,1,0:T(8,128)(2,1)} %bitcast.2, bf16[4,8,576]{2,1,0:T(8,128)(2,1)} %new_ref.1, bf16[4,512,128]{2,1,0:T(8,128)(2,1)} %vu_hbm.1, ...), custom_call_target="tpu_custom_call" | custom-call | tf_op jit(solution)/shard_map/pallas_call | solution.py:510
  144.2 1.8 %copy.10 = bf16[4,8,7168]{2,1,0:T(8,128)(2,1)} copy(bf16[4,8,7168]{2,1,0:T(8,128)(2,1)} %shard_map.82) | data formatting | bytes 917504
